TPU v7x, 32 devices: a whole 2x2x4 slice. The times are simulated.
32 devices in a mesh: grp: 2 (over y), row: 8 (over z, x), col: 2 (over core).
Axes of the slice: x: 2, y: 2, z: 4, core: 2. Of those that a mesh axis runs over, the one named last changes fastest.
Arguments:
- potential: float32 [128, 32, 128], P(('grp', 'row')), parts along dimension 0, may hold values from -6 to 6
- charges_guess: float32 [128, 32, 128], P(('grp', 'row')), parts along dimension 0, may hold values from -4 to 4
- elast_diag: bfloat16 [128, 128, 128], P(('grp', 'row')), parts along dimension 0, as said below
- elast_off: bfloat16 [128, 14, 128, 128], P(('grp', 'row'), 'col'), parts along dimension 0, may hold values from -0.03125 to 0.03125
- factor_diag: bfloat16 [128, 128, 128], P(('grp', 'row')), parts along dimension 0, as said below
- factor_off: bfloat16 [128, 14, 128, 128], P(('grp', 'row'), 'col'), parts along dimension 0, may hold values from -0.0234375 to 0.0234375
- block_slot: int32 [128, 14], P(('grp', 'row'), 'col'), parts along dimension 0, may hold values from 0 to 55, as said below
- need_list: int32 [16, 2, 7, 8], P(('grp', 'row'), 'col'), parts along dimension 0, may hold values from 0 to 7, as said below
Outputs:
- charges: float32 [128, 32, 128], P(('grp', 'row')), parts along dimension 0
- residual: float32 [128, 32, 128], P(('grp', 'row')), parts along dimension 0
There are 2 independent parts, one for each index of `grp`. A program takes and returns all parts, laid end to end along the dimension named above; each array names one. Nothing has to cross between parts.
Inputs may be any that keep to these rules, and one draw needn't show every extreme that they name: `block_slot`: within one device's 8 x 7 slots all positions differ; position t * 8 + j stands for entry j of need_list[s, c, t] with s = (d + t - 3) mod 8. need_list[s, c, t] holds 8 distinct block rows of row index s, numbered within that index. `elast_diag`: each block is symmetric, with diagonal entries near 1.2 to 2.4 and other entries under 0.6 / sqrt(128) in size. `factor_diag`: diagonal entries near 0.6 to 1.0, other entries under 0.6 / sqrt(128) in size.
All inputs are finite; a program needn't handle non-finite values.
Results may differ from a plain program's by a relative error of at most 0.015.
The roundings to bfloat16 on the way count: a program that leaves them out, or rounds other values in their place, can miss the bound.
Values may be sent and summed in bfloat16 or wider, within the bound.
A program may use at most 64 MiB of HBM per device.

v0:
```python
import jax
import jax.numpy as jnp
from jax import lax
from jax.sharding import PartitionSpec as P

ITERS = 3


def shifted(value, axis, steps):
    count = lax.axis_size(axis)
    pairs = [(source, (source + steps) % count) for source in range(count)]
    return lax.ppermute(value, axis, pairs)


def local(
    potential, charges_guess, elast_diag, elast_off, factor_diag, factor_off, block_slot, need_list
):
    near_count = need_list.shape[2]
    list_width = need_list.shape[3]
    reach = (near_count - 1) // 2
    send_rows = need_list.reshape(near_count * list_width)
    slot_list = block_slot.reshape(-1)
    block_rows, slot_count = block_slot.shape
    rhs_count, atom_count = (potential.shape[1], potential.shape[2])

    def panels_of(vector_bf):
        return vector_bf[send_rows].reshape(near_count, list_width, rhs_count, atom_count)

    def ghosts_of(arrived):
        flat = arrived.reshape(near_count * list_width, rhs_count, atom_count)
        return flat[slot_list].reshape(block_rows, slot_count, rhs_count, atom_count)

    def forward_of(off_blocks, ghost_blocks):
        return jnp.einsum(
            "bkij,bkrj->bri", off_blocks, ghost_blocks, preferred_element_type=jnp.float32
        )

    def outgoing_of(off_blocks, vector_bf):
        contribution = jnp.einsum(
            "bkij,bri->bkrj", off_blocks, vector_bf, preferred_element_type=jnp.float32
        )
        outgoing = jnp.zeros((near_count * list_width, rhs_count, atom_count), jnp.float32)
        outgoing = outgoing.at[slot_list].add(contribution.reshape(-1, rhs_count, atom_count))
        return outgoing.astype(jnp.bfloat16).reshape(near_count, list_width, rhs_count, atom_count)

    def landed(arrived):
        flat = arrived.astype(jnp.float32).reshape(-1, rhs_count, atom_count)
        return jnp.zeros((block_rows, rhs_count, atom_count), jnp.float32).at[send_rows].add(flat)

    def fetch(vector_bf):
        panels = panels_of(vector_bf)
        pieces = []
        for offset_slot in range(near_count):
            offset = offset_slot - reach
            if offset == 0:
                pieces.append(panels[offset_slot])
            else:
                pieces.append(shifted(panels[offset_slot], "row", -offset))
        return ghosts_of(jnp.stack(pieces))

    def give_back(outgoing):
        pieces = []
        for offset_slot in range(near_count):
            offset = offset_slot - reach
            if offset == 0:
                pieces.append(outgoing[offset_slot])
            else:
                pieces.append(shifted(outgoing[offset_slot], "row", offset))
        return landed(jnp.stack(pieces))

    def across(partial_part):
        return lax.psum(partial_part, "col")

    def elast_parts(vector):
        vector_bf = vector.astype(jnp.bfloat16)
        ghost_blocks = fetch(vector_bf)
        returned = give_back(outgoing_of(elast_off, vector_bf))
        off_part = forward_of(elast_off, ghost_blocks) + returned
        diag_part = jnp.einsum(
            "bij,brj->bri", elast_diag, vector_bf, preferred_element_type=jnp.float32
        )
        return (off_part, diag_part)

    def factor_parts(vector):
        vector_bf = vector.astype(jnp.bfloat16)
        inner_w = across(forward_of(factor_off, fetch(vector_bf)))
        inner_w = inner_w + jnp.einsum(
            "bij,brj->bri", factor_diag, vector_bf, preferred_element_type=jnp.float32
        )
        inner_bf = inner_w.astype(jnp.bfloat16)
        off_part = give_back(outgoing_of(factor_off, inner_bf))
        diag_part = jnp.einsum(
            "bji,brj->bri", factor_diag, inner_bf, preferred_element_type=jnp.float32
        )
        return (off_part, diag_part)

    def combined(other, off_part, diag_part):
        full_vector = across(off_part) + diag_part
        product = lax.psum(jnp.sum(other * full_vector, axis=(0, 2)), "row")
        return (full_vector, product)

    start_off, start_diag = elast_parts(charges_guess)
    residual = potential - (across(start_off) + start_diag)
    pre_off, pre_diag = factor_parts(residual)
    precond, rz_value = combined(residual, pre_off, pre_diag)
    direction = precond
    charges = charges_guess
    for sweep_index in range(ITERS):
        image_off, image_diag = elast_parts(direction)
        image, curvature = combined(direction, image_off, image_diag)
        step_size = rz_value / curvature
        charges = charges + step_size[None, :, None] * direction
        residual = residual - step_size[None, :, None] * image
        if sweep_index + 1 < ITERS:
            pre_off, pre_diag = factor_parts(residual)
            precond, fresh = combined(residual, pre_off, pre_diag)
            direction = precond + (fresh / rz_value)[None, :, None] * direction
            rz_value = fresh
    return (charges, residual)


def solution(mesh):
    return jax.shard_map(
        local,
        mesh=mesh,
        in_specs=(
            P(("grp", "row"), None, None),
            P(("grp", "row"), None, None),
            P(("grp", "row"), None, None),
            P(("grp", "row"), "col", None, None),
            P(("grp", "row"), None, None),
            P(("grp", "row"), "col", None, None),
            P(("grp", "row"), "col"),
            P(("grp", "row"), "col", None, None),
        ),
        out_specs=(P(("grp", "row"), None, None), P(("grp", "row"), None, None)),
        check_vma=False,
    )
```

profile of v0, /device:TPU:0, one launch (start us, length us, event | category | flops | bytes accessed | tf_op | source)
XLA Modules:
  0.0 638.7 jit_solution(945178830266618547)
XLA Ops:
  22.1 6.1 scatter_fusion
  54.4 16.9 %all-reduce.12.cloned.1.call-done = f32[8,32,128]{2,1,0:T(8,128)} async-done(((f32[8,32,128]{2,1,0:T(8,128)}), f32[8,32,128]{2,1,0:T(8,128)}) %all-reduce.12.cloned.1.call-update) | async-done | bytes 131088 | tf_op jit(solution)/shard_map/psum | solution.py:72
  92.1 19.4 %all-reduce.14.cloned.1.call-done = f32[8,32,128]{2,1,0:T(8,128)} async-done(((f32[8,32,128]{2,1,0:T(8,128)}), f32[8,32,128]{2,1,0:T(8,128)}) %all-reduce.14.cloned.1.call-update) | async-done | bytes 131088 | tf_op jit(solution)/shard_map/psum | solution.py:72
  115.6 6.1 scatter_fusion.2
  140.6 20.2 %all-reduce.16.cloned.1.call-done = f32[8,32,128]{2,1,0:T(8,128)} async-done(((f32[8,32,128]{2,1,0:T(8,128)}), f32[8,32,128]{2,1,0:T(8,128)}) %all-reduce.16.cloned.1.call-update) | async-done | bytes 131088 | tf_op jit(solution)/shard_map/psum | solution.py:72
  165.5 6.1 scatter_fusion.4
  207.6 18.3 %all-reduce.18.cloned.1.call-done = f32[8,32,128]{2,1,0:T(8,128)} async-done(((f32[8,32,128]{2,1,0:T(8,128)}), f32[8,32,128]{2,1,0:T(8,128)}) %all-reduce.18.cloned.1.call-update) | async-done | bytes 131088 | tf_op jit(solution)/shard_map/psum | solution.py:72
  227.2 21.6 %all-reduce = (f32[32]{0:T(128)S(1)}, f32[32]{0:T(128)S(1)}) all-reduce(f32[32]{0:T(128)S(1)} %get-tuple-element.3, f32[32]{0:T(128)S(1)} %get-tuple-element.2), channel_id=1, replica_groups=mesh['grp'=2,'row'=8,'col'=2] {'row'}, use_global_device_ids=true, to_apply=%region_8.0 | all-reduce | flops 64 | bytes 512 | tf_op jit(solution)/shard_map/psum | solution.py:99
  268.5 15.9 %all-reduce.20.cloned.1.call-done = f32[8,32,128]{2,1,0:T(8,128)} async-done(((f32[8,32,128]{2,1,0:T(8,128)}), f32[8,32,128]{2,1,0:T(8,128)}) %all-reduce.20.cloned.1.call-update) | async-done | bytes 131088 | tf_op jit(solution)/shard_map/psum | solution.py:72
  288.6 6.1 scatter_fusion.6
  313.7 20.2 %all-reduce.22.cloned.1.call-done = f32[8,32,128]{2,1,0:T(8,128)} async-done(((f32[8,32,128]{2,1,0:T(8,128)}), f32[8,32,128]{2,1,0:T(8,128)}) %all-reduce.22.cloned.1.call-update) | async-done | bytes 131088 | tf_op jit(solution)/shard_map/psum | solution.py:72
  335.2 21.6 %psum.120 = f32[32]{0:T(128)S(1)} all-reduce(f32[32]{0:T(128)S(1)} %get-tuple-element.103), channel_id=1, replica_groups=mesh['grp'=2,'row'=8,'col'=2] {'row'}, use_global_device_ids=true, to_apply=%region_19.0 | all-reduce | flops 32 | bytes 256 | tf_op jit(solution)/shard_map/psum | solution.py:99
  361.1 6.1 scatter_fusion.8
  380.1 4.2 collective-permute-start.51
  400.6 16.5 %all-reduce.24.cloned.1.call-done = f32[8,32,128]{2,1,0:T(8,128)} async-done(((f32[8,32,128]{2,1,0:T(8,128)}), f32[8,32,128]{2,1,0:T(8,128)}) %all-reduce.24.cloned.1.call-update) | async-done | bytes 131088 | tf_op jit(solution)/shard_map/psum | solution.py:72
  418.5 21.6 %psum.122 = f32[32]{0:T(128)S(1)} all-reduce(f32[32]{0:T(128)S(1)} %get-tuple-element.105), channel_id=1, replica_groups=mesh['grp'=2,'row'=8,'col'=2] {'row'}, use_global_device_ids=true, to_apply=%region_24.0 | all-reduce | flops 32 | bytes 256 | tf_op jit(solution)/shard_map/psum | solution.py:99
  459.4 15.7 %all-reduce.26.cloned.1.call-done = f32[8,32,128]{2,1,0:T(8,128)} async-done(((f32[8,32,128]{2,1,0:T(8,128)}), f32[8,32,128]{2,1,0:T(8,128)}) %all-reduce.26.cloned.1.call-update) | async-done | bytes 131088 | tf_op jit(solution)/shard_map/psum | solution.py:72
  479.3 6.1 scatter_fusion.10
  504.3 20.2 %all-reduce.28.cloned.1.call-done = f32[8,32,128]{2,1,0:T(8,128)} async-done(((f32[8,32,128]{2,1,0:T(8,128)}), f32[8,32,128]{2,1,0:T(8,128)}) %all-reduce.28.cloned.1.call-update) | async-done | bytes 131088 | tf_op jit(solution)/shard_map/psum | solution.py:72
  525.8 21.6 %psum.125 = f32[32]{0:T(128)S(1)} all-reduce(f32[32]{0:T(128)S(1)} %get-tuple-element.107), channel_id=1, replica_groups=mesh['grp'=2,'row'=8,'col'=2] {'row'}, use_global_device_ids=true, to_apply=%region_30.0 | all-reduce | flops 32 | bytes 256 | tf_op jit(solution)/shard_map/psum | solution.py:99
  551.0 6.1 scatter_fusion.12
  570.0 4.2 collective-permute-start.75
  590.5 16.6 %all-reduce.30.cloned.1.call-done = f32[8,32,128]{2,1,0:T(8,128)} async-done(((f32[8,32,128]{2,1,0:T(8,128)}), f32[8,32,128]{2,1,0:T(8,128)}) %all-reduce.30.cloned.1.call-update) | async-done | bytes 131088 | tf_op jit(solution)/shard_map/psum | solution.py:72
  608.4 21.6 %psum.127 = f32[32]{0:T(128)S(1)} all-reduce(f32[32]{0:T(128)S(1)} %get-tuple-element.109), channel_id=1, replica_groups=mesh['grp'=2,'row'=8,'col'=2] {'row'}, use_global_device_ids=true, to_apply=%region_35.0 | all-reduce | flops 32 | bytes 256 | tf_op jit(solution)/shard_map/psum | solution.py:99
  (451 shorter events, 284.2 us)
Async XLA Ops:
  7.2 64.1 %all-reduce.12.cloned.1.call-start = ((), (), s32[]{:S(2)}) async-start(), calls=%async_computation | async-start | bytes 262144 | tf_op jit(solution)/shard_map/psum | solution.py:72
  9.8 18.6 %collective-permute-start = (bf16[8,32,128]{2,1,0:T(8,128)(2,1)S(1)}, bf16[8,32,128]{2,1,0:T(8,128)(2,1)}, u32[]{:S(2)}, u32[]{:S(2)}) collective-permute-start(bf16[8,32,128]{2,1,0:T(8,128)(2,1)S(1)} %get-tuple-element.95), channel_id=1, source_target_pairs={{0,6},{2,8},{4,10},{6,12},{8,14},{10,0},{12,2},{14,4},{1,7},{3,9},... | collective-permute-start | bytes 196616 | tf_op jit(solution)/shard_map/ppermute | solution.py:12
  13.8 15.5 %collective-permute-start.1 = (bf16[8,32,128]{2,1,0:T(8,128)(2,1)S(1)}, bf16[8,32,128]{2,1,0:T(8,128)(2,1)}, u32[]{:S(2)}, u32[]{:S(2)}) collective-permute-start(bf16[8,32,128]{2,1,0:T(8,128)(2,1)S(1)} %get-tuple-element.94), channel_id=1, source_target_pairs={{0,4},{2,6},{4,8},{6,10},{8,12},{10,14},{12,0},{14,2},{1,5},{3,7},... | collective-permute-start | bytes 196616 | tf_op jit(solution)/shard_map/ppermute | solution.py:12
  15.4 18.7 %collective-permute-start.2 = (bf16[8,32,128]{2,1,0:T(8,128)(2,1)S(1)}, bf16[8,32,128]{2,1,0:T(8,128)(2,1)}, u32[]{:S(2)}, u32[]{:S(2)}) collective-permute-start(bf16[8,32,128]{2,1,0:T(8,128)(2,1)S(1)} %get-tuple-element.93), channel_id=1, source_target_pairs={{0,2},{2,4},{4,6},{6,8},{8,10},{10,12},{12,14},{14,0},{1,3},{3,5},... | collective-permute-start | bytes 196616 | tf_op jit(solution)/shard_map/ppermute | solution.py:12
  16.9 25.7 %collective-permute-start.3 = (bf16[8,32,128]{2,1,0:T(8,128)(2,1)S(1)}, bf16[8,32,128]{2,1,0:T(8,128)(2,1)S(1)}, u32[]{:S(2)}, u32[]{:S(2)}) collective-permute-start(bf16[8,32,128]{2,1,0:T(8,128)(2,1)S(1)} %get-tuple-element.92), channel_id=1, source_target_pairs={{0,14},{2,0},{4,2},{6,4},{8,6},{10,8},{12,10},{14,12},{1,15},{3,1}... | collective-permute-start | bytes 196616 | tf_op jit(solution)/shard_map/ppermute | solution.py:12
  20.1 25.0 %collective-permute-start.4 = (bf16[8,32,128]{2,1,0:T(8,128)(2,1)S(1)}, bf16[8,32,128]{2,1,0:T(8,128)(2,1)S(1)}, u32[]{:S(2)}, u32[]{:S(2)}) collective-permute-start(bf16[8,32,128]{2,1,0:T(8,128)(2,1)S(1)} %get-tuple-element.91), channel_id=1, source_target_pairs={{0,12},{2,14},{4,0},{6,2},{8,4},{10,6},{12,8},{14,10},{1,13},{3,15... | collective-permute-start | bytes 196616 | tf_op jit(solution)/shard_map/ppermute | solution.py:12
  28.3 16.8 %collective-permute-start.5 = (bf16[8,32,128]{2,1,0:T(8,128)(2,1)S(1)}, bf16[8,32,128]{2,1,0:T(8,128)(2,1)S(1)}, u32[]{:S(2)}, u32[]{:S(2)}) collective-permute-start(bf16[8,32,128]{2,1,0:T(8,128)(2,1)S(1)} %get-tuple-element.90), channel_id=1, source_target_pairs={{0,10},{2,12},{4,14},{6,0},{8,2},{10,4},{12,6},{14,8},{1,11},{3,13... | collective-permute-start | bytes 196616 | tf_op jit(solution)/shard_map/ppermute | solution.py:12
  54.4 57.1 %all-reduce.14.cloned.1.call-start = ((), (), s32[]{:S(2)}) async-start(), calls=%async_computation.1 | async-start | bytes 262144 | tf_op jit(solution)/shard_map/psum | solution.py:72
  92.0 68.8 %all-reduce.16.cloned.1.call-start = ((), (), s32[]{:S(2)}) async-start(), calls=%async_computation.2 | async-start | bytes 262144 | tf_op jit(solution)/shard_map/psum | solution.py:72
  140.6 85.3 %all-reduce.18.cloned.1.call-start = ((), (), s32[]{:S(2)}) async-start(), calls=%async_computation.3 | async-start | bytes 262144 | tf_op jit(solution)/shard_map/psum | solution.py:72
  179.4 12.9 %collective-permute-start.35 = (bf16[8,32,128]{2,1,0:T(8,128)(2,1)S(1)}, bf16[8,32,128]{2,1,0:T(8,128)(2,1)S(1)}, u32[]{:S(2)}, u32[]{:S(2)}) collective-permute-start(bf16[8,32,128]{2,1,0:T(8,128)(2,1)S(1)} %get-tuple-element.60), channel_id=1, source_target_pairs={{0,6},{2,8},{4,10},{6,12},{8,14},{10,0},{12,2},{14,4},{1,7},{3,9},... | collective-permute-start | bytes 196616 | tf_op jit(solution)/shard_map/ppermute | solution.py:12
  181.3 11.8 %collective-permute-start.24 = (bf16[8,32,128]{2,1,0:T(8,128)(2,1)S(1)}, bf16[8,32,128]{2,1,0:T(8,128)(2,1)S(1)}, u32[]{:S(2)}, u32[]{:S(2)}) collective-permute-start(bf16[8,32,128]{2,1,0:T(8,128)(2,1)S(1)} %get-tuple-element.71), channel_id=1, source_target_pairs={{0,6},{2,8},{4,10},{6,12},{8,14},{10,0},{12,2},{14,4},{1,7},{3,9},... | collective-permute-start | bytes 196616 | tf_op jit(solution)/shard_map/ppermute | solution.py:12
  184.8 11.5 %collective-permute-start.26 = (bf16[8,32,128]{2,1,0:T(8,128)(2,1)S(1)}, bf16[8,32,128]{2,1,0:T(8,128)(2,1)S(1)}, u32[]{:S(2)}, u32[]{:S(2)}) collective-permute-start(bf16[8,32,128]{2,1,0:T(8,128)(2,1)S(1)} %get-tuple-element.69), channel_id=1, source_target_pairs={{0,2},{2,4},{4,6},{6,8},{8,10},{10,12},{12,14},{14,0},{1,3},{3,5},... | collective-permute-start | bytes 196616 | tf_op jit(solution)/shard_map/ppermute | solution.py:12
  207.6 76.9 %all-reduce.20.cloned.1.call-start = ((), (), s32[]{:S(2)}) async-start(), calls=%async_computation.4 | async-start | bytes 262144 | tf_op jit(solution)/shard_map/psum | solution.py:72
  268.5 65.4 %all-reduce.22.cloned.1.call-start = ((), (), s32[]{:S(2)}) async-start(), calls=%async_computation.5 | async-start | bytes 262144 | tf_op jit(solution)/shard_map/psum | solution.py:72
  313.6 103.5 %all-reduce.24.cloned.1.call-start = ((), (), s32[]{:S(2)}) async-start(), calls=%async_computation.6 | async-start | bytes 262144 | tf_op jit(solution)/shard_map/psum | solution.py:72
  367.5 11.9 %collective-permute-start.56 = (bf16[8,32,128]{2,1,0:T(8,128)(2,1)S(1)}, bf16[8,32,128]{2,1,0:T(8,128)(2,1)S(1)}, u32[]{:S(2)}, u32[]{:S(2)}) collective-permute-start(bf16[8,32,128]{2,1,0:T(8,128)(2,1)S(1)} %get-tuple-element.39), channel_id=1, source_target_pairs={{0,14},{2,0},{4,2},{6,4},{8,6},{10,8},{12,10},{14,12},{1,15},{3,1}... | collective-permute-start | bytes 196616 | tf_op jit(solution)/shard_map/ppermute | solution.py:12
  373.6 10.7 %collective-permute-start.59 = (bf16[8,32,128]{2,1,0:T(8,128)(2,1)S(1)}, bf16[8,32,128]{2,1,0:T(8,128)(2,1)S(1)}, u32[]{:S(2)}, u32[]{:S(2)}) collective-permute-start(bf16[8,32,128]{2,1,0:T(8,128)(2,1)S(1)} %get-tuple-element.36), channel_id=1, source_target_pairs={{0,6},{2,8},{4,10},{6,12},{8,14},{10,0},{12,2},{14,4},{1,7},{3,9},... | collective-permute-start | bytes 196616 | tf_op jit(solution)/shard_map/ppermute | solution.py:12
  375.4 11.2 %collective-permute-start.48 = (bf16[8,32,128]{2,1,0:T(8,128)(2,1)S(1)}, bf16[8,32,128]{2,1,0:T(8,128)(2,1)S(1)}, u32[]{:S(2)}, u32[]{:S(2)}) collective-permute-start(bf16[8,32,128]{2,1,0:T(8,128)(2,1)S(1)} %get-tuple-element.47), channel_id=1, source_target_pairs={{0,6},{2,8},{4,10},{6,12},{8,14},{10,0},{12,2},{14,4},{1,7},{3,9},... | collective-permute-start | bytes 196616 | tf_op jit(solution)/shard_map/ppermute | solution.py:12
  400.6 74.5 %all-reduce.26.cloned.1.call-start = ((), (), s32[]{:S(2)}) async-start(), calls=%async_computation.7 | async-start | bytes 262144 | tf_op jit(solution)/shard_map/psum | solution.py:72
  459.1 65.4 %all-reduce.28.cloned.1.call-start = ((), (), s32[]{:S(2)}) async-start(), calls=%async_computation.8 | async-start | bytes 262144 | tf_op jit(solution)/shard_map/psum | solution.py:72
  504.3 102.8 %all-reduce.30.cloned.1.call-start = ((), (), s32[]{:S(2)}) async-start(), calls=%async_computation.9 | async-start | bytes 262144 | tf_op jit(solution)/shard_map/psum | solution.py:72
  557.4 11.9 %collective-permute-start.80 = (bf16[8,32,128]{2,1,0:T(8,128)(2,1)S(1)}, bf16[8,32,128]{2,1,0:T(8,128)(2,1)S(1)}, u32[]{:S(2)}, u32[]{:S(2)}) collective-permute-start(bf16[8,32,128]{2,1,0:T(8,128)(2,1)S(1)} %get-tuple-element.15), channel_id=1, source_target_pairs={{0,14},{2,0},{4,2},{6,4},{8,6},{10,8},{12,10},{14,12},{1,15},{3,1}... | collective-permute-start | bytes 196616 | tf_op jit(solution)/shard_map/ppermute | solution.py:12
  565.3 11.2 %collective-permute-start.72 = (bf16[8,32,128]{2,1,0:T(8,128)(2,1)S(1)}, bf16[8,32,128]{2,1,0:T(8,128)(2,1)S(1)}, u32[]{:S(2)}, u32[]{:S(2)}) collective-permute-start(bf16[8,32,128]{2,1,0:T(8,128)(2,1)S(1)} %get-tuple-element.23), channel_id=1, source_target_pairs={{0,6},{2,8},{4,10},{6,12},{8,14},{10,0},{12,2},{14,4},{1,7},{3,9},... | collective-permute-start | bytes 196616 | tf_op jit(solution)/shard_map/ppermute | solution.py:12
  (103 other events, 927.4 us)
Sparse Core Ops, SparseCore 0:
  54.5 16.7 all-reduce.11
  92.1 19.2 all-reduce.13
  140.7 20.1 all-reduce.15
  207.7 18.1 all-reduce.17
  268.6 15.8 all-reduce.19
  313.7 20.1 all-reduce.21
  400.7 16.3 all-reduce.23
  459.2 15.8 all-reduce.25
  504.4 20.1 all-reduce.27
  590.7 16.3 all-reduce.29
where the time goes:
time: 641 us; the launch traced here: 639 us
  waiting for transfers between devices  225 us (35%)
  starting transfers between devices  129 us (20%)
  blocking collectives  108 us (17%)
  other arithmetic  76.4 us (12%)
  matrix products  42.4 us (7%)
  local copies, waits for them, and re-layouts  41.9 us (7%)
  between operations  15.5 us (2%)
    psum x10, waiting for transfers between devices, across(): return lax.psum(partial_part, 'col')  180 us
    ppermute x84, starting transfers between devices, shifted(): return lax.ppermute(value, axis, pairs)  128 us
    psum x5, blocking collectives, combined(): product = lax.psum(jnp.sum(other * full_vector, axis=(0, 2)), 'row')  108 us
    ppermute x84, waiting for transfers between devices, shifted(): return lax.ppermute(value, axis, pairs)  45.3 us
    scatter-add x7, other arithmetic, outgoing_of(): outgoing.at[slot_list].add(contribution.reshape(-1, rhs_count, atom_count))  42.6 us
    scatter-add x7, other arithmetic, landed(): jnp.zeros((block_rows, rhs_count, atom_count), jnp.float32).at[send_rows]  23.4 us
    unnamed x150, local copies, waits for them, and re-layouts  22.1 us
    dot_general x7, matrix products, forward_of(): jnp.einsum('bkij,bkrj->bri', off_blocks, ghost_blocks, preferred_element_...  14.7 us
  transfers between devices with their start and end apart: 94, of which 37 were waited for; matrix products, arithmetic and copies ran while one was open for 4% of the time, Pallas kernels for 0%

commit v1 on v0

v1 whole, which is shorter than its diff:
```python
import functools

import jax
import jax.numpy as jnp
from jax import lax
from jax.experimental import pallas as pl
from jax.experimental.pallas import tpu as pltpu
from jax.sharding import PartitionSpec as P

ITERS = 3
F32 = jnp.float32
BF16 = jnp.bfloat16


def mm(a, b):
    return lax.dot_general(a, b, (((1,), (0,)), ((), ())), preferred_element_type=F32)


def mm_t(a, b):
    return lax.dot_general(a, b, (((1,), (1,)), ((), ())), preferred_element_type=F32)


def kernel(
    rows_n, near, half,
    take_ref, brow_ref, pot_ref, guess_ref, ediag_ref, eoff_ref, fdiag_ref, foff_ref,
    charges_ref, resid_ref,
    w_ref, stage_ref, ghost_ref, full_ref, rout_ref, rin_ref, pout_ref, pin_ref, ar_ref,
    w_send, w_recv, g_send, g_recv, f_send, f_recv, r_send, r_recv, p_send, p_recv,
    a_send, a_recv, o_send, o_recv,
):
    d = lax.axis_index("row")
    h = lax.axis_index("col")
    sib = 1 - h
    reach = (near - 1) // 2
    group = rows_n * 2
    me = d * 2 + h
    rhs, atoms = pot_ref.shape[1], pot_ref.shape[2]
    per = near * half
    mine = pl.ds(h * half, half)
    theirs = pl.ds(sib * half, half)

    barrier = pltpu.get_barrier_semaphore()

    def greet(o, c):
        other = lax.rem(me + o, group)
        pl.semaphore_signal(
            barrier, inc=1, device_id={"row": other // 2, "col": lax.rem(other, 2)},
            device_id_type=pl.DeviceIdType.MESH)
        return c

    lax.fori_loop(1, group, greet, 0)

    def pick_other(m, off_ref):
        def body(n, c):
            stage_ref[m, n] = off_ref[take_ref[per + n]]
            return c
        lax.fori_loop(0, per, body, 0)

    def pick_own(m, off_ref):
        def body(n, c):
            w_ref[m, 0, n] = off_ref[take_ref[n]]
            return c
        lax.fori_loop(0, per, body, 0)

    def remote(src, dst, ssem, rsem, row, col):
        return pltpu.make_async_remote_copy(
            src_ref=src, dst_ref=dst, send_sem=ssem, recv_sem=rsem,
            device_id={"row": row, "col": col}, device_id_type=pl.DeviceIdType.MESH)

    def weights(m):
        return remote(stage_ref.at[m], w_ref.at[m, 1], w_send.at[m], w_recv.at[m], d, sib)

    pick_other(0, eoff_ref)
    pl.semaphore_wait(barrier, group - 1)
    weights(0).start()

    def order(q):
        return reach + (1 - 2 * lax.rem(q, 2)) * ((q + 1) // 2)

    def ghost_copy(e, t):
        row = lax.rem(d + reach - t + rows_n, rows_n)
        return remote(ghost_ref.at[e, reach], ghost_ref.at[e, t], g_send.at[e, t], g_recv.at[e, t], row, h)

    def full_copy(e):
        return remote(full_ref.at[e, mine], full_ref.at[e, mine], f_send.at[e], f_recv.at[e], d, sib)

    def ret_copy(e, t):
        row = lax.rem(d + t - reach + rows_n, rows_n)
        return remote(rout_ref.at[e, t], rin_ref.at[e, t], r_send.at[e, t], r_recv.at[e, t], row, h)

    def part_copy(e):
        return remote(pout_ref.at[e, theirs], pin_ref.at[e], p_send.at[e], p_recv.at[e], d, sib)

    def loop_q(body):
        def step(q, c):
            body(order(q))
            return c
        lax.fori_loop(1, near, step, 0)

    def fetch_start(e, vb):
        ghost_ref[e, reach] = vb
        loop_q(lambda t: ghost_copy(e, t).start())

    def transposed(e):
        def one(t):
            for r in range(half):
                n = t * half + r
                first = mm(full_ref[e, brow_ref[n]], w_ref[e, 0, n]).astype(BF16).astype(F32)
                second = mm(full_ref[e, brow_ref[per + n]], w_ref[e, 1, n]).astype(BF16).astype(F32)
                rout_ref[e, t, r] = (first + second).astype(BF16)

        def far(t):
            one(t)
            ret_copy(e, t).start()
        loop_q(far)
        one(reach)

    def forward(e):
        blocks = 2 * half

        def one(t, acc):
            acc = list(acc)
            for r in range(half):
                n = t * half + r
                both = jnp.concatenate([w_ref[e, 0, n], w_ref[e, 1, n]], axis=0)
                got = mm_t(ghost_ref[e, t, r], both)
                for side in range(2):
                    piece = got[:, side * atoms:(side + 1) * atoms]
                    b = brow_ref[side * per + n]
                    for row in range(blocks):
                        acc[row] = acc[row] + jnp.where(b == row, piece, 0.0)
            return tuple(acc)

        acc = one(reach, tuple(jnp.zeros((rhs, atoms), F32) for _ in range(blocks)))

        def step(q, acc):
            t = order(q)
            ghost_copy(e, t).wait_recv()
            return one(t, acc)

        acc = lax.fori_loop(1, near, step, acc)
        for row in range(blocks):
            pout_ref[e, row] = acc[row]
        part_copy(e).start()

    def diag(ref, vb, transpose):
        out = []
        for r in range(half):
            block = ref[h * half + r]
            out.append(mm(vb[r], block) if transpose else mm_t(vb[r], block))
        return jnp.stack(out)

    def returned(e):
        total = rout_ref[e, reach].astype(F32)
        for q in range(1, near):
            t = reach + (1 - 2 * (q % 2)) * ((q + 1) // 2)
            ret_copy(e, t).wait_recv()
            total = total + rin_ref[e, t].astype(F32)
        return total

    def drain(e):
        def one(t):
            ghost_copy(e, t).wait_send()
            ret_copy(e, t).wait_send()
        loop_q(one)
        full_copy(e).wait_send()
        part_copy(e).wait_send()

    def elast(v):
        e = 0
        vb = v.astype(BF16)
        full_ref[e, mine] = vb
        full_copy(e).start()
        fetch_start(e, vb)
        return vb

    def elast_end(vb):
        e = 0
        full_copy(e).wait_recv()
        transposed(e)
        dpart = diag(ediag_ref, vb, False)
        forward(e)
        total = dpart + returned(e)
        part_copy(e).wait_recv()
        total = total + (pout_ref[e, mine] + pin_ref[e])
        drain(e)
        return total

    def factor(v, after_start=None):
        e = 1
        vb = v.astype(BF16)
        fetch_start(e, vb)
        if after_start is not None:
            after_start()
        dpart = diag(fdiag_ref, vb, False)
        forward(e)
        part_copy(e).wait_recv()
        w = dpart + (pout_ref[e, mine] + pin_ref[e])
        wb = w.astype(BF16)
        full_ref[e, mine] = wb
        full_copy(e).start()
        dpart = diag(fdiag_ref, wb, True)
        full_copy(e).wait_recv()
        transposed(e)
        total = dpart + returned(e)
        drain(e)
        return total

    count = [0]

    def dot(a, b):
        par = count[0] % 2
        count[0] += 1
        s = jnp.sum(a * b, axis=0)
        s = jnp.concatenate([s, jnp.zeros((atoms - rhs, atoms), F32)], axis=0)
        ar_ref[par, 0] = jnp.sum(s.T, axis=0, keepdims=True)

        def copy(o):
            other = lax.rem(me + o, group)
            return remote(ar_ref.at[par, 0], ar_ref.at[par, o], a_send.at[par, o], a_recv.at[par, o],
                          other // 2, lax.rem(other, 2))

        def start(o, c):
            copy(o).start()
            return c

        def finish(o, c):
            copy(o).wait()
            return c

        lax.fori_loop(1, group, start, 0)
        lax.fori_loop(1, group, finish, 0)
        total = jnp.sum(ar_ref[par], axis=0)
        return jnp.broadcast_to(total, (atoms, atoms)).T[:rhs]

    guess = guess_ref[mine]
    vb = elast(guess)
    pick_own(0, eoff_ref)
    pick_other(1, foff_ref)
    weights(1).start()
    pick_own(1, foff_ref)
    weights(0).wait()
    residual = pot_ref[mine] - elast_end(vb)
    precond = factor(residual, lambda: weights(1).wait())
    rz = dot(residual, precond)
    resid_ref[mine] = residual
    charges_ref[mine] = guess
    direction = precond
    for sweep in range(ITERS):
        image = elast_end(elast(direction))
        step = rz / dot(direction, image)
        charges_ref[mine] = charges_ref[mine] + step[None] * direction
        residual = resid_ref[mine] - step[None] * image
        resid_ref[mine] = residual
        if sweep + 1 < ITERS:
            precond = factor(residual)
            fresh = dot(residual, precond)
            direction = precond + (fresh / rz)[None] * direction
            rz = fresh
    last = [
        remote(ref.at[mine], ref.at[mine], o_send.at[i], o_recv.at[i], d, sib)
        for i, ref in enumerate((charges_ref, resid_ref))
    ]
    for copy in last:
        copy.start()
    for copy in last:
        copy.wait()


def local(
    potential, charges_guess, elast_diag, elast_off, factor_diag, factor_off, block_slot, need_list
):
    rows_n = lax.axis_size("row")
    near, width = need_list.shape[2], need_list.shape[3]
    reach = (near - 1) // 2
    block_rows, slot_count = block_slot.shape
    rhs, atoms = potential.shape[1], potential.shape[2]
    slots = block_rows * slot_count
    assert slots == near * width and width == block_rows and lax.axis_size("col") == 2
    half = block_rows // 2
    per = near * half
    d = lax.axis_index("row")
    h = lax.axis_index("col")

    flat = block_slot.reshape(-1)
    i32 = jnp.int32
    slot_at = jnp.sum(
        jnp.where(flat[None, :] == jnp.arange(slots, dtype=i32)[:, None], jnp.arange(slots, dtype=i32)[None, :], 0),
        axis=1)
    needs = need_list[0, 0]
    at = jnp.arange(width, dtype=i32)
    place = jnp.sum(jnp.where(needs[:, None, :] == at[None, :, None], at[None, None, :], 0), axis=2)
    both = jnp.concatenate([slot_at, place.reshape(-1)])
    every = lax.all_gather(both, ("row", "col")).reshape(rows_n, 2, 2 * slots)
    wrapped = jnp.concatenate([every[-reach:], every, every[:reach]], axis=0) if rows_n > 1 else every
    window = lax.dynamic_slice_in_dim(wrapped, d, near, axis=0)
    slot_both = lax.dynamic_index_in_dim(every, d, axis=0, keepdims=False)[:, :slots]
    ids = jnp.arange(near)
    place_both = window[:, :, slots:].reshape(near, 2, near, width)[ids, :, ids].transpose(1, 0, 2)
    pos = place_both + (jnp.arange(near, dtype=i32) * width)[None, :, None]
    pos = pos.reshape(2, slots)
    hit = pos[:, :, None] == jnp.arange(slots, dtype=i32)[None, None, :]
    item = jnp.sum(jnp.where(hit, slot_both[:, None, :], 0), axis=2).reshape(2, near, 2, half)
    own = jnp.where(h == 0, item[0], item[1])
    other = jnp.where(h == 0, item[1], item[0])

    def in_half(x, which):
        return jnp.where(which == 0, x[:, 0], x[:, 1]).reshape(-1)

    take = jnp.concatenate([in_half(own, h), in_half(own, 1 - h)])
    brow = jnp.concatenate([in_half(own, h), in_half(other, h)]) // slot_count

    vmem = pl.BlockSpec(memory_space=pltpu.VMEM)
    smem = pl.BlockSpec(memory_space=pltpu.SMEM)
    group = rows_n * 2
    dma = pltpu.SemaphoreType.DMA
    shape = jax.ShapeDtypeStruct(potential.shape, F32)
    return pl.pallas_call(
        functools.partial(kernel, rows_n, near, half),
        out_shape=(shape, shape),
        in_specs=[smem, smem] + [vmem] * 6,
        out_specs=(vmem, vmem),
        scratch_shapes=[
            pltpu.VMEM((2, 2, per, atoms, atoms), BF16),
            pltpu.VMEM((2, per, atoms, atoms), BF16),
            pltpu.VMEM((2, near, half, rhs, atoms), BF16),
            pltpu.VMEM((2, block_rows, rhs, atoms), BF16),
            pltpu.VMEM((2, near, half, rhs, atoms), BF16),
            pltpu.VMEM((2, near, half, rhs, atoms), BF16),
            pltpu.VMEM((2, block_rows, rhs, atoms), F32),
            pltpu.VMEM((2, half, rhs, atoms), F32),
            pltpu.VMEM((2, group, 1, atoms), F32),
            dma((2,)), dma((2,)),
            dma((2, near)), dma((2, near)),
            dma((2,)), dma((2,)),
            dma((2, near)), dma((2, near)),
            dma((2,)), dma((2,)),
            dma((2, group)), dma((2, group)),
            dma((2,)), dma((2,)),
        ],
        compiler_params=pltpu.CompilerParams(
            collective_id=0, has_side_effects=True, vmem_limit_bytes=48 * 1024 * 1024),
    )(
        take, brow, potential, charges_guess, elast_diag,
        elast_off.reshape(slots, atoms, atoms), factor_diag, factor_off.reshape(slots, atoms, atoms),
    )


def solution(mesh):
    return jax.shard_map(
        local,
        mesh=mesh,
        in_specs=(
            P(("grp", "row"), None, None),
            P(("grp", "row"), None, None),
            P(("grp", "row"), None, None),
            P(("grp", "row"), "col", None, None),
            P(("grp", "row"), None, None),
            P(("grp", "row"), "col", None, None),
            P(("grp", "row"), "col"),
            P(("grp", "row"), "col", None, None),
        ),
        out_specs=(P(("grp", "row"), None, None), P(("grp", "row"), None, None)),
        check_vma=False,
    )
```

time: 641 us -> 148 us (0.23)
  waiting for transfers between devices: 225 us -> 0 us
  starting transfers between devices: 129 us -> 0 us
  Pallas kernels: 0 us -> 119 us
  blocking collectives: 108 us -> 13.9 us
  other arithmetic: 76.4 us -> 1.01 us
  matrix products: 42.4 us -> 0 us
  local copies, waits for them, and re-layouts: 41.9 us -> 12.3 us
  between operations: 15.5 us -> 1.4 us
    psum x10 -> x0, waiting for transfers between devices: 180 us -> none  [across(): return lax.psum(partial_part, 'col')]
    ppermute x84 -> x0, starting transfers between devices: 128 us -> none  [shifted(): return lax.ppermute(value, axis, pairs)]
    pallas_call x0 -> x1, Pallas kernels: none -> 119 us  [local(): pl.pallas_call(functools.partial(kernel, rows_n, near, half), out_shape=(...]
    psum x5 -> x0, blocking collectives: 108 us -> none  [combined(): product = lax.psum(jnp.sum(other * full_vector, axis=(0, 2)), 'row')]
    scatter-add x14 -> x0, other arithmetic: 65.9 us -> none  [the longest x7 42.6 us: outgoing_of(): outgoing.at[slot_list].add(contribution.reshape(-1, rhs_count, atom_count))]
    ppermute x84 -> x0, waiting for transfers between devices: 45.3 us -> none  [shifted(): return lax.ppermute(value, axis, pairs)]
    dot_general x24 -> x0, matrix products: 42.4 us -> none  [the longest x7 14.7 us: forward_of(): jnp.einsum('bkij,bkrj->bri', off_blocks, ghost_blocks, preferred_element_...]
    gather x14 -> x1, local copies, waits for them, and re-layouts: 16.6 us -> 0.61 us  [local(): window[:, :, slots:].reshape(near, 2, near, width)[ids, :, ids]]
  transfers between devices with their start and end apart: 94 -> 0, of which waited for: 37 -> 0; matrix products, arithmetic and copies ran while one was open for 4% -> 0% of each run, Pallas kernels for 0% -> 0%
where the time goes in v1:
time: 148 us
  Pallas kernels  119 us (80%)
  blocking collectives  13.9 us (9%)
  local copies, waits for them, and re-layouts  12.3 us (8%)
    pallas_call x1, Pallas kernels, local(): pl.pallas_call(functools.partial(kernel, rows_n, near, half), out_shape=(...  119 us
    unnamed x1, blocking collectives  13.9 us
    unnamed x17, local copies, waits for them, and re-layouts  9.95 us

profile of v1, /device:TPU:0, one launch (start us, length us, event | category | flops | bytes accessed | tf_op | source)
XLA Modules:
  0.0 147.6 jit_solution(18290826681666369702)
XLA Ops:
  0.6 1.2 dynamic-slice
  2.5 0.8 eq.56
  3.3 0.1 select_reduce_fusion.2
  3.4 0.7 copy.16
  4.1 0.2 select_reduce_fusion.1
  4.4 0.2 add_dynamic-update-slice_fusion
  4.6 13.9 %all-reduce = s32[1792]{0:T(1024)S(1)} all-reduce(s32[1792]{0:T(1024)S(1)} %add_dynamic-update-slice_fusion), channel_id=2, replica_groups=mesh['grp'=2,'row'=8,'col'=2] {'row','col'}, use_global_device_ids=true, to_apply=%add | all-reduce | flops 1792 | bytes 14336
  18.5 0.1 reshape.55
  18.8 0.1 fusion.1
  18.9 0.1 reshape.56
  19.0 0.6 gather_fusion
  19.8 0.2 select_reduce_fusion
  20.0 0.1 select_n.91
  20.1 0.1 select_n.84
  20.5 0.1 and_select_fusion
  20.6 1.5 %copy-done = bf16[8,7,128,128]{3,2,1,0:T(8,128)(2,1)S(1)} copy-done((bf16[8,7,128,128]{3,2,1,0:T(8,128)(2,1)S(1)}, bf16[8,7,128,128]{3,2,1,0:T(8,128)(2,1)}, u32[]{:S(2)}) %copy-start) | copy-done | bytes 1835032
  22.1 1.5 %copy-done.1 = bf16[8,7,128,128]{3,2,1,0:T(8,128)(2,1)S(1)} copy-done((bf16[8,7,128,128]{3,2,1,0:T(8,128)(2,1)S(1)}, bf16[8,7,128,128]{3,2,1,0:T(8,128)(2,1)}, u32[]{:S(2)}) %copy-start.1) | copy-done | bytes 1835032
  23.6 0.9 copy-done.2
  24.6 0.9 copy-done.3
  25.5 0.9 copy-done.4
  26.4 0.9 copy-done.5
  27.3 118.9 %shard_map.95 = (f32[8,32,128]{2,1,0:T(8,128)S(1)}, f32[8,32,128]{2,1,0:T(8,128)S(1)}) custom-call(s32[56]{0:T(128)S(1)} %get-tuple-element.9.take_ref, s32[56]{0:T(128)S(1)} %get-tuple-element.8.brow_ref, f32[8,32,128]{2,1,0:T(8,128)S(1)} %copy-done.4, f32[8,32,128]{2,1,0:T(8,128)S(1)} %copy-done.5, bf16[8,128,128]{2,1,0:T(8,128)(2,1)S(1)} %copy-done.2, ...), custom_call_target="tpu_custom_call" | custom-call | tf_op jit(solution)/shard_map/pallas_call | solution.py:318
  146.3 0.7 copy.20
  146.9 0.7 copy.21
  (23 shorter events, 0.8 us)
Async XLA Ops:
  20.6 1.5 %copy-start = (bf16[8,7,128,128]{3,2,1,0:T(8,128)(2,1)S(1)}, bf16[8,7,128,128]{3,2,1,0:T(8,128)(2,1)}, u32[]{:S(2)}) copy-start(bf16[8,7,128,128]{3,2,1,0:T(8,128)(2,1)} %param.11) | copy-start | bytes 5505028
  22.1 1.5 %copy-start.1 = (bf16[8,7,128,128]{3,2,1,0:T(8,128)(2,1)S(1)}, bf16[8,7,128,128]{3,2,1,0:T(8,128)(2,1)}, u32[]{:S(2)}) copy-start(bf16[8,7,128,128]{3,2,1,0:T(8,128)(2,1)} %param.13) | copy-start | bytes 5505028
  23.6 0.9 copy-start.2
  24.6 0.9 copy-start.3
  25.5 0.9 copy-start.4
  26.4 0.9 copy-start.5

commit v2 on v1

--- a/solution.py
+++ b/solution.py
@@ -22,12 +22,16 @@
 
 def kernel(
     rows_n, near, half,
-    take_ref, brow_ref, pot_ref, guess_ref, ediag_ref, eoff_ref, fdiag_ref, foff_ref,
+    slot_ref, need_ref, pot_hbm, guess_hbm, ediag_hbm, eoff_hbm, fdiag_hbm, foff_hbm,
     charges_ref, resid_ref,
-    w_ref, stage_ref, ghost_ref, full_ref, rout_ref, rin_ref, pout_ref, pin_ref, ar_ref,
+    take_ref, brow_ref, msg_ref, list_ref, table_ref,
+    pot_ref, guess_ref, ediag_ref, eoff_ref, fdiag_ref, foff_ref,
+    in_sem, m_send, m_recv, t_sem,
+    w_ref, stage_ref, ghost_ref, full_e_ref, full_f_ref, rout_ref, rin_ref, pout_ref, pin_ref, ar_ref,
     w_send, w_recv, g_send, g_recv, f_send, f_recv, r_send, r_recv, p_send, p_recv,
     a_send, a_recv, o_send, o_recv,
 ):
+    full_refs = (full_e_ref, full_f_ref)
     d = lax.axis_index("row")
     h = lax.axis_index("col")
     sib = 1 - h
@@ -39,6 +43,15 @@
     mine = pl.ds(h * half, half)
     theirs = pl.ds(sib * half, half)
 
+    loads = [
+        pltpu.make_async_copy(src, dst, in_sem.at[i])
+        for i, (src, dst) in enumerate((
+            (guess_hbm, guess_ref), (eoff_hbm, eoff_ref), (foff_hbm, foff_ref),
+            (pot_hbm, pot_ref), (ediag_hbm, ediag_ref), (fdiag_hbm, fdiag_ref)))
+    ]
+    for load in loads:
+        load.start()
+
     barrier = pltpu.get_barrier_semaphore()
 
     def greet(o, c):
@@ -70,9 +83,58 @@
     def weights(m):
         return remote(stage_ref.at[m], w_ref.at[m, 1], w_send.at[m], w_recv.at[m], d, sib)
 
-    pick_other(0, eoff_ref)
+    block_rows, slot_count = slot_ref.shape
+    width = need_ref.shape[1]
+    lane = lax.broadcasted_iota(jnp.int32, (block_rows, atoms), 1)
+    line = lax.broadcasted_iota(jnp.int32, (block_rows, atoms), 0)
+    slot_at = jnp.zeros((block_rows, atoms), jnp.int32)
+    for k in range(slot_count):
+        slot_at = slot_at + jnp.where(slot_ref[:, k:k + 1] == lane, line * slot_count + k, 0)
+    slot_at = jnp.sum(slot_at, axis=0, keepdims=True)
+    lane = lax.broadcasted_iota(jnp.int32, (near, atoms), 1)
+    place = jnp.zeros((near, atoms), jnp.int32)
+    for j in range(width):
+        place = place + jnp.where(need_ref[:, j:j + 1] == lane, j, 0)
+    msg_ref[0, reach] = jnp.concatenate([place, slot_at], axis=0)
+
+    def msg_copy(k, t):
+        row = lax.rem(d + reach - t + rows_n, rows_n)
+        return remote(msg_ref.at[0, reach], msg_ref.at[k, t], m_send.at[k, t], m_recv.at[k, t],
+                      row, lax.rem(h + k, 2))
+
+    messages = [(k, t) for k in range(2) for t in range(near) if (k, t) != (0, reach)]
+
+    def read_lists():
+        for k, t in messages:
+            msg_copy(k, t).wait()
+        list_ref[...] = jnp.concatenate(
+            [line for k in range(2)
+             for line in [msg_ref[k, t, t:t + 1] for t in range(near)] + [msg_ref[k, reach, near:near + 1]]],
+            axis=0)
+        copy = pltpu.make_async_copy(list_ref, table_ref, t_sem.at[0])
+        copy.start()
+        copy.wait()
+
+        def fill(n, c):
+            t = n // half
+            r = lax.rem(n, half)
+
+            def slot_of(k, side):
+                at = jnp.clip(table_ref[k * (near + 1) + t, side * half + r], 0, width - 1)
+                return jnp.clip(table_ref[k * (near + 1) + near, t * width + at], 0, 2 * per - 1)
+
+            own = slot_of(0, h)
+            take_ref[n] = own
+            take_ref[per + n] = slot_of(0, sib)
+            brow_ref[n] = own // slot_count
+            brow_ref[per + n] = slot_of(1, h) // slot_count
+            return c
+
+        lax.fori_loop(0, per, fill, 0)
+
     pl.semaphore_wait(barrier, group - 1)
-    weights(0).start()
+    for k, t in messages:
+        msg_copy(k, t).start()
 
     def order(q):
         return reach + (1 - 2 * lax.rem(q, 2)) * ((q + 1) // 2)
@@ -82,7 +144,7 @@
         return remote(ghost_ref.at[e, reach], ghost_ref.at[e, t], g_send.at[e, t], g_recv.at[e, t], row, h)
 
     def full_copy(e):
-        return remote(full_ref.at[e, mine], full_ref.at[e, mine], f_send.at[e], f_recv.at[e], d, sib)
+        return remote(full_refs[e].at[mine], full_refs[e].at[mine], f_send.at[e], f_recv.at[e], d, sib)
 
     def ret_copy(e, t):
         row = lax.rem(d + t - reach + rows_n, rows_n)
@@ -105,8 +167,8 @@
         def one(t):
             for r in range(half):
                 n = t * half + r
-                first = mm(full_ref[e, brow_ref[n]], w_ref[e, 0, n]).astype(BF16).astype(F32)
-                second = mm(full_ref[e, brow_ref[per + n]], w_ref[e, 1, n]).astype(BF16).astype(F32)
+                first = mm(full_refs[e][brow_ref[n]], w_ref[e, 0, n]).astype(BF16).astype(F32)
+                second = mm(full_refs[e][brow_ref[per + n]], w_ref[e, 1, n]).astype(BF16).astype(F32)
                 rout_ref[e, t, r] = (first + second).astype(BF16)
 
         def far(t):
@@ -169,22 +231,25 @@
     def elast(v):
         e = 0
         vb = v.astype(BF16)
-        full_ref[e, mine] = vb
+        full_refs[e][mine] = vb
         full_copy(e).start()
         fetch_start(e, vb)
         return vb
 
-    def elast_end(vb):
+    def elast_end(vb, v=None):
         e = 0
         full_copy(e).wait_recv()
         transposed(e)
         dpart = diag(ediag_ref, vb, False)
         forward(e)
-        total = dpart + returned(e)
         part_copy(e).wait_recv()
-        total = total + (pout_ref[e, mine] + pin_ref[e])
+        stored = pout_ref[e, mine] + pin_ref[e]
+        finish = None
+        if v is not None:
+            finish = dot_start(jnp.sum(v * (dpart + 2.0 * stored), axis=0))
+        total = dpart + stored + returned(e)
         drain(e)
-        return total
+        return total if finish is None else (total, finish())
 
     def factor(v, after_start=None):
         e = 1
@@ -197,21 +262,21 @@
         part_copy(e).wait_recv()
         w = dpart + (pout_ref[e, mine] + pin_ref[e])
         wb = w.astype(BF16)
-        full_ref[e, mine] = wb
+        full_refs[e][mine] = wb
         full_copy(e).start()
+        finish = dot_start(jnp.sum(w * wb.astype(F32), axis=0))
         dpart = diag(fdiag_ref, wb, True)
         full_copy(e).wait_recv()
         transposed(e)
         total = dpart + returned(e)
         drain(e)
-        return total
+        return total, finish()
 
     count = [0]
 
-    def dot(a, b):
+    def dot_start(s):
         par = count[0] % 2
         count[0] += 1
-        s = jnp.sum(a * b, axis=0)
         s = jnp.concatenate([s, jnp.zeros((atoms - rhs, atoms), F32)], axis=0)
         ar_ref[par, 0] = jnp.sum(s.T, axis=0, keepdims=True)
 
@@ -229,32 +294,41 @@
             return c
 
         lax.fori_loop(1, group, start, 0)
-        lax.fori_loop(1, group, finish, 0)
-        total = jnp.sum(ar_ref[par], axis=0)
-        return jnp.broadcast_to(total, (atoms, atoms)).T[:rhs]
-
+        def end():
+            lax.fori_loop(1, group, finish, 0)
+            total = jnp.sum(ar_ref[par], axis=0)
+            return jnp.broadcast_to(total, (atoms, atoms)).T[:rhs]
+
+        return end
+
+    loads[0].wait()
     guess = guess_ref[mine]
     vb = elast(guess)
+    read_lists()
+    loads[1].wait()
+    pick_other(0, eoff_ref)
+    weights(0).start()
+    loads[2].wait()
     pick_own(0, eoff_ref)
     pick_other(1, foff_ref)
     weights(1).start()
     pick_own(1, foff_ref)
+    for load in loads[3:]:
+        load.wait()
     weights(0).wait()
     residual = pot_ref[mine] - elast_end(vb)
-    precond = factor(residual, lambda: weights(1).wait())
-    rz = dot(residual, precond)
+    precond, rz = factor(residual, lambda: weights(1).wait())
     resid_ref[mine] = residual
     charges_ref[mine] = guess
     direction = precond
     for sweep in range(ITERS):
-        image = elast_end(elast(direction))
-        step = rz / dot(direction, image)
+        image, curvature = elast_end(elast(direction), direction)
+        step = rz / curvature
         charges_ref[mine] = charges_ref[mine] + step[None] * direction
         residual = resid_ref[mine] - step[None] * image
         resid_ref[mine] = residual
         if sweep + 1 < ITERS:
-            precond = factor(residual)
-            fresh = dot(residual, precond)
+            precond, fresh = factor(residual)
             direction = precond + (fresh / rz)[None] * direction
             rz = fresh
     last = [
@@ -279,52 +353,30 @@
     assert slots == near * width and width == block_rows and lax.axis_size("col") == 2
     half = block_rows // 2
     per = near * half
-    d = lax.axis_index("row")
-    h = lax.axis_index("col")
-
-    flat = block_slot.reshape(-1)
-    i32 = jnp.int32
-    slot_at = jnp.sum(
-        jnp.where(flat[None, :] == jnp.arange(slots, dtype=i32)[:, None], jnp.arange(slots, dtype=i32)[None, :], 0),
-        axis=1)
-    needs = need_list[0, 0]
-    at = jnp.arange(width, dtype=i32)
-    place = jnp.sum(jnp.where(needs[:, None, :] == at[None, :, None], at[None, None, :], 0), axis=2)
-    both = jnp.concatenate([slot_at, place.reshape(-1)])
-    every = lax.all_gather(both, ("row", "col")).reshape(rows_n, 2, 2 * slots)
-    wrapped = jnp.concatenate([every[-reach:], every, every[:reach]], axis=0) if rows_n > 1 else every
-    window = lax.dynamic_slice_in_dim(wrapped, d, near, axis=0)
-    slot_both = lax.dynamic_index_in_dim(every, d, axis=0, keepdims=False)[:, :slots]
-    ids = jnp.arange(near)
-    place_both = window[:, :, slots:].reshape(near, 2, near, width)[ids, :, ids].transpose(1, 0, 2)
-    pos = place_both + (jnp.arange(near, dtype=i32) * width)[None, :, None]
-    pos = pos.reshape(2, slots)
-    hit = pos[:, :, None] == jnp.arange(slots, dtype=i32)[None, None, :]
-    item = jnp.sum(jnp.where(hit, slot_both[:, None, :], 0), axis=2).reshape(2, near, 2, half)
-    own = jnp.where(h == 0, item[0], item[1])
-    other = jnp.where(h == 0, item[1], item[0])
-
-    def in_half(x, which):
-        return jnp.where(which == 0, x[:, 0], x[:, 1]).reshape(-1)
-
-    take = jnp.concatenate([in_half(own, h), in_half(own, 1 - h)])
-    brow = jnp.concatenate([in_half(own, h), in_half(other, h)]) // slot_count
-
     vmem = pl.BlockSpec(memory_space=pltpu.VMEM)
-    smem = pl.BlockSpec(memory_space=pltpu.SMEM)
+    hbm = pl.BlockSpec(memory_space=pltpu.HBM)
     group = rows_n * 2
     dma = pltpu.SemaphoreType.DMA
     shape = jax.ShapeDtypeStruct(potential.shape, F32)
     return pl.pallas_call(
         functools.partial(kernel, rows_n, near, half),
         out_shape=(shape, shape),
-        in_specs=[smem, smem] + [vmem] * 6,
+        in_specs=[vmem] * 2 + [hbm] * 6,
         out_specs=(vmem, vmem),
         scratch_shapes=[
+            pltpu.SMEM((slots,), jnp.int32), pltpu.SMEM((slots,), jnp.int32),
+            pltpu.VMEM((2, near, near + 1, atoms), jnp.int32),
+            pltpu.VMEM((2 * (near + 1), atoms), jnp.int32),
+            pltpu.SMEM((2 * (near + 1), atoms), jnp.int32),
+            pltpu.VMEM(potential.shape, F32), pltpu.VMEM(potential.shape, F32),
+            pltpu.VMEM(elast_diag.shape, BF16), pltpu.VMEM((slots, atoms, atoms), BF16),
+            pltpu.VMEM(elast_diag.shape, BF16), pltpu.VMEM((slots, atoms, atoms), BF16),
+            dma((6,)), dma((2, near)), dma((2, near)), dma((1,)),
             pltpu.VMEM((2, 2, per, atoms, atoms), BF16),
             pltpu.VMEM((2, per, atoms, atoms), BF16),
             pltpu.VMEM((2, near, half, rhs, atoms), BF16),
-            pltpu.VMEM((2, block_rows, rhs, atoms), BF16),
+            pltpu.VMEM((block_rows, rhs, atoms), BF16),
+            pltpu.VMEM((block_rows, rhs, atoms), BF16),
             pltpu.VMEM((2, near, half, rhs, atoms), BF16),
             pltpu.VMEM((2, near, half, rhs, atoms), BF16),
             pltpu.VMEM((2, block_rows, rhs, atoms), F32),
@@ -341,7 +393,7 @@
         compiler_params=pltpu.CompilerParams(
             collective_id=0, has_side_effects=True, vmem_limit_bytes=48 * 1024 * 1024),
     )(
-        take, brow, potential, charges_guess, elast_diag,
+        block_slot, need_list.reshape(near, width), potential, charges_guess, elast_diag,
         elast_off.reshape(slots, atoms, atoms), factor_diag, factor_off.reshape(slots, atoms, atoms),
     )
 

time: 148 us -> 121 us (0.82)
  blocking collectives: 13.9 us -> 0 us
  Pallas kernels: 119 us -> 110 us
  local copies, waits for them, and re-layouts: 12.3 us -> 9.39 us
    unnamed x1 -> x0, blocking collectives: 13.9 us -> none
    pallas_call x1, Pallas kernels: 119 us -> 110 us  [local(): pl.pallas_call(functools.partial(kernel, rows_n, near, half), out_shape=(...]
where the time goes in v2:
time: 121 us; the launch traced here: 120 us
  Pallas kernels  110 us (91%)
  local copies, waits for them, and re-layouts  9.39 us (8%)
    pallas_call x1, Pallas kernels, local(): pl.pallas_call(functools.partial(kernel, rows_n, near, half), out_shape=(...  110 us
    unnamed x17, local copies, waits for them, and re-layouts  9.39 us

profile of v2, /device:TPU:0, one launch (start us, length us, event | category | flops | bytes accessed | tf_op | source)
XLA Modules:
  0.0 120.4 jit_solution(11333742629817138115)
XLA Ops:
  0.6 0.7 copy.12
  1.3 0.0 copy-start
  1.3 1.5 %copy-done = bf16[8,7,128,128]{3,2,1,0:T(8,128)(2,1)S(1)} copy-done((bf16[8,7,128,128]{3,2,1,0:T(8,128)(2,1)S(1)}, bf16[8,7,128,128]{3,2,1,0:T(8,128)(2,1)}, u32[]{:S(2)}) %copy-start) | copy-done | bytes 1835032
  2.8 0.0 copy-start.1
  2.8 1.5 %copy-done.1 = bf16[8,7,128,128]{3,2,1,0:T(8,128)(2,1)S(1)} copy-done((bf16[8,7,128,128]{3,2,1,0:T(8,128)(2,1)S(1)}, bf16[8,7,128,128]{3,2,1,0:T(8,128)(2,1)}, u32[]{:S(2)}) %copy-start.1) | copy-done | bytes 1835032
  4.3 0.0 copy-start.2
  4.3 0.9 copy-done.2
  5.3 0.0 copy-start.3
  5.3 0.9 copy-done.3
  6.2 0.0 copy-start.4
  6.2 0.9 copy-done.4
  7.1 0.0 copy-start.5
  7.1 0.9 copy-done.5
  8.0 0.0 copy-start.6
  8.0 0.7 copy-done.6
  8.7 110.4 %shard_map.95 = (f32[8,32,128]{2,1,0:T(8,128)S(1)}, f32[8,32,128]{2,1,0:T(8,128)S(1)}) custom-call(s32[8,7]{1,0:T(8,128)S(1)} %copy-done.6, s32[7,8]{1,0:T(8,128)S(1)} %bitcast.7, f32[8,32,128]{2,1,0:T(8,128)S(1)} %copy-done.4, f32[8,32,128]{2,1,0:T(8,128)S(1)} %copy-done.5, bf16[8,128,128]{2,1,0:T(8,128)(2,1)S(1)} %copy-done.2, ...), custom_call_target="tpu_custom_call" | custom-call | tf_op jit(solution)/shard_map/pallas_call | solution.py:361
  119.1 0.7 copy.15
  119.8 0.7 copy.16
Async XLA Ops:
  1.3 1.5 %copy-start = (bf16[8,7,128,128]{3,2,1,0:T(8,128)(2,1)S(1)}, bf16[8,7,128,128]{3,2,1,0:T(8,128)(2,1)}, u32[]{:S(2)}) copy-start(bf16[8,7,128,128]{3,2,1,0:T(8,128)(2,1)} %param.11) | copy-start | bytes 5505028
  2.8 1.5 %copy-start.1 = (bf16[8,7,128,128]{3,2,1,0:T(8,128)(2,1)S(1)}, bf16[8,7,128,128]{3,2,1,0:T(8,128)(2,1)}, u32[]{:S(2)}) copy-start(bf16[8,7,128,128]{3,2,1,0:T(8,128)(2,1)} %param.13) | copy-start | bytes 5505028
  4.3 0.9 copy-start.2
  5.3 0.9 copy-start.3
  6.2 0.9 copy-start.4
  7.1 0.9 copy-start.5
  8.0 0.7 copy-start.6

commit v3 on v2

--- a/solution.py
+++ b/solution.py
@@ -37,7 +37,6 @@
     sib = 1 - h
     reach = (near - 1) // 2
     group = rows_n * 2
-    me = d * 2 + h
     rhs, atoms = pot_ref.shape[1], pot_ref.shape[2]
     per = near * half
     mine = pl.ds(h * half, half)
@@ -54,14 +53,30 @@
 
     barrier = pltpu.get_barrier_semaphore()
 
-    def greet(o, c):
-        other = lax.rem(me + o, group)
+    def wrap(x):
+        return jnp.where(x < 0, x + rows_n, jnp.where(x >= rows_n, x - rows_n, x))
+
+    cols = (h, sib)
+
+    def each_other(body):
+        body(0, 1, d, sib)
+        if rows_n <= 8:
+            for o in range(1, rows_n):
+                for k in range(2):
+                    body(o, k, wrap(d + o), cols[k])
+        else:
+            def step(o, c):
+                for k in range(2):
+                    body(o, k, wrap(d + o), cols[k])
+                return c
+            lax.fori_loop(1, rows_n, step, 0)
+
+    def greet(o, k, row, col):
         pl.semaphore_signal(
-            barrier, inc=1, device_id={"row": other // 2, "col": lax.rem(other, 2)},
+            barrier, inc=1, device_id={"row": row, "col": col},
             device_id_type=pl.DeviceIdType.MESH)
-        return c
-
-    lax.fori_loop(1, group, greet, 0)
+
+    each_other(greet)
 
     def pick_other(m, off_ref):
         def body(n, c):
@@ -87,9 +102,10 @@
     width = need_ref.shape[1]
     lane = lax.broadcasted_iota(jnp.int32, (block_rows, atoms), 1)
     line = lax.broadcasted_iota(jnp.int32, (block_rows, atoms), 0)
+    pad = 1 << (slot_count - 1).bit_length()
     slot_at = jnp.zeros((block_rows, atoms), jnp.int32)
     for k in range(slot_count):
-        slot_at = slot_at + jnp.where(slot_ref[:, k:k + 1] == lane, line * slot_count + k, 0)
+        slot_at = slot_at + jnp.where(slot_ref[:, k:k + 1] == lane, line * pad + k, 0)
     slot_at = jnp.sum(slot_at, axis=0, keepdims=True)
     lane = lax.broadcasted_iota(jnp.int32, (near, atoms), 1)
     place = jnp.zeros((near, atoms), jnp.int32)
@@ -98,9 +114,9 @@
     msg_ref[0, reach] = jnp.concatenate([place, slot_at], axis=0)
 
     def msg_copy(k, t):
-        row = lax.rem(d + reach - t + rows_n, rows_n)
+        row = wrap(d + reach - t)
         return remote(msg_ref.at[0, reach], msg_ref.at[k, t], m_send.at[k, t], m_recv.at[k, t],
-                      row, lax.rem(h + k, 2))
+                      row, cols[k])
 
     messages = [(k, t) for k in range(2) for t in range(near) if (k, t) != (0, reach)]
 
@@ -115,53 +131,50 @@
         copy.start()
         copy.wait()
 
-        def fill(n, c):
-            t = n // half
-            r = lax.rem(n, half)
-
-            def slot_of(k, side):
-                at = jnp.clip(table_ref[k * (near + 1) + t, side * half + r], 0, width - 1)
-                return jnp.clip(table_ref[k * (near + 1) + near, t * width + at], 0, 2 * per - 1)
-
-            own = slot_of(0, h)
-            take_ref[n] = own
-            take_ref[per + n] = slot_of(0, sib)
-            brow_ref[n] = own // slot_count
-            brow_ref[per + n] = slot_of(1, h) // slot_count
-            return c
-
-        lax.fori_loop(0, per, fill, 0)
+        def slot_of(k, t, side, r):
+            at = jnp.clip(table_ref[k * (near + 1) + t, side * half + r], 0, width - 1)
+            code = table_ref[k * (near + 1) + near, t * width + at]
+            row = jnp.clip(lax.shift_right_arithmetic(code, shift), 0, block_rows - 1)
+            return jnp.clip(code - row * (pad - slot_count), 0, 2 * per - 1), row
+
+        shift = pad.bit_length() - 1
+        for t in range(near):
+            for r in range(half):
+                n = t * half + r
+                take_ref[n], brow_ref[n] = slot_of(0, t, h, r)
+                take_ref[per + n] = slot_of(0, t, sib, r)[0]
+                brow_ref[per + n] = slot_of(1, t, h, r)[1]
 
     pl.semaphore_wait(barrier, group - 1)
     for k, t in messages:
         msg_copy(k, t).start()
 
-    def order(q):
-        return reach + (1 - 2 * lax.rem(q, 2)) * ((q + 1) // 2)
-
     def ghost_copy(e, t):
-        row = lax.rem(d + reach - t + rows_n, rows_n)
+        row = wrap(d + reach - t)
         return remote(ghost_ref.at[e, reach], ghost_ref.at[e, t], g_send.at[e, t], g_recv.at[e, t], row, h)
 
     def full_copy(e):
         return remote(full_refs[e].at[mine], full_refs[e].at[mine], f_send.at[e], f_recv.at[e], d, sib)
 
     def ret_copy(e, t):
-        row = lax.rem(d + t - reach + rows_n, rows_n)
+        row = wrap(d + t - reach)
         return remote(rout_ref.at[e, t], rin_ref.at[e, t], r_send.at[e, t], r_recv.at[e, t], row, h)
 
     def part_copy(e):
         return remote(pout_ref.at[e, theirs], pin_ref.at[e], p_send.at[e], p_recv.at[e], d, sib)
 
     def loop_q(body):
-        def step(q, c):
-            body(order(q))
+        def step(i, c):
+            body(reach - i)
+            body(reach + i)
             return c
-        lax.fori_loop(1, near, step, 0)
+        lax.fori_loop(1, reach + 1, step, 0)
 
     def fetch_start(e, vb):
         ghost_ref[e, reach] = vb
-        loop_q(lambda t: ghost_copy(e, t).start())
+        for i in range(1, reach + 1):
+            ghost_copy(e, reach - i).start()
+            ghost_copy(e, reach + i).start()
 
     def transposed(e):
         def one(t):
@@ -195,12 +208,13 @@
 
         acc = one(reach, tuple(jnp.zeros((rhs, atoms), F32) for _ in range(blocks)))
 
-        def step(q, acc):
-            t = order(q)
-            ghost_copy(e, t).wait_recv()
-            return one(t, acc)
-
-        acc = lax.fori_loop(1, near, step, acc)
+        def step(i, acc):
+            for t in (reach - i, reach + i):
+                ghost_copy(e, t).wait_recv()
+                acc = one(t, acc)
+            return acc
+
+        acc = lax.fori_loop(1, reach + 1, step, acc)
         for row in range(blocks):
             pout_ref[e, row] = acc[row]
         part_copy(e).start()
@@ -280,22 +294,14 @@
         s = jnp.concatenate([s, jnp.zeros((atoms - rhs, atoms), F32)], axis=0)
         ar_ref[par, 0] = jnp.sum(s.T, axis=0, keepdims=True)
 
-        def copy(o):
-            other = lax.rem(me + o, group)
-            return remote(ar_ref.at[par, 0], ar_ref.at[par, o], a_send.at[par, o], a_recv.at[par, o],
-                          other // 2, lax.rem(other, 2))
-
-        def start(o, c):
-            copy(o).start()
-            return c
-
-        def finish(o, c):
-            copy(o).wait()
-            return c
-
-        lax.fori_loop(1, group, start, 0)
+        def copy(o, k, row, col):
+            at = o * 2 + k
+            return remote(ar_ref.at[par, 0], ar_ref.at[par, at], a_send.at[par, at], a_recv.at[par, at], row, col)
+
+        each_other(lambda *to: copy(*to).start())
+
         def end():
-            lax.fori_loop(1, group, finish, 0)
+            each_other(lambda *to: copy(*to).wait())
             total = jnp.sum(ar_ref[par], axis=0)
             return jnp.broadcast_to(total, (atoms, atoms)).T[:rhs]
 
@@ -391,7 +397,7 @@
             dma((2,)), dma((2,)),
         ],
         compiler_params=pltpu.CompilerParams(
-            collective_id=0, has_side_effects=True, vmem_limit_bytes=48 * 1024 * 1024),
+            collective_id=0, has_side_effects=True, vmem_limit_bytes=63 * 1024 * 1024),
     )(
         block_slot, need_list.reshape(near, width), potential, charges_guess, elast_diag,
         elast_off.reshape(slots, atoms, atoms), factor_diag, factor_off.reshape(slots, atoms, atoms),

time: 121 us -> 114 us (0.942)
  local copies, waits for them, and re-layouts: 9.39 us -> 4.41 us
  Pallas kernels: 110 us -> 108 us
    unnamed x17 -> x3, local copies, waits for them, and re-layouts: 9.39 us -> 4.41 us
    pallas_call x1, Pallas kernels: 110 us -> 108 us  [local(): pl.pallas_call(functools.partial(kernel, rows_n, near, half), out_shape=(...]
where the time goes in v3:
time: 114 us; the launch traced here: 113 us
  Pallas kernels  108 us (95%)
  local copies, waits for them, and re-layouts  4.41 us (4%)
    pallas_call x1, Pallas kernels, local(): pl.pallas_call(functools.partial(kernel, rows_n, near, half), out_shape=(...  108 us
    unnamed x3, local copies, waits for them, and re-layouts  4.41 us

profile of v3, /device:TPU:0, one launch (start us, length us, event | category | flops | bytes accessed | tf_op | source)
XLA Modules:
  0.0 113.3 jit_solution(14797920923793661109)
XLA Ops:
  0.6 1.3 %copy.12 = s32[1,1,7,8]{3,2,1,0:T(8,128)} copy(s32[1,1,7,8]{3,1,2,0:T(1,128)} %param.15) | data formatting | bytes 448
  1.9 108.3 %shard_map.95 = (f32[8,32,128]{2,1,0:T(8,128)}, f32[8,32,128]{2,1,0:T(8,128)}) custom-call(s32[8,7]{1,0:T(8,128)} %slot_ref.1, s32[7,8]{1,0:T(8,128)} %bitcast.7, f32[8,32,128]{2,1,0:T(8,128)} %pot_hbm.1, f32[8,32,128]{2,1,0:T(8,128)} %guess_hbm.1, bf16[8,128,128]{2,1,0:T(8,128)(2,1)} %ediag_hbm.1, bf16[56,128,128]{2,1,0:T(8,128)(2,1)} %bitcast.5, ...), custom_call_target="tpu_custom_call" | custom-call | tf_op jit(solution)/shard_map/pallas_call | solution.py:367
  110.2 1.6 %copy.15 = f32[8,32,128]{2,1,0:T(8,128)} copy(f32[8,32,128]{2,1,0:T(8,128)} %get-tuple-element.4) | data formatting | bytes 262144
  111.7 1.6 %copy.16 = f32[8,32,128]{2,1,0:T(8,128)} copy(f32[8,32,128]{2,1,0:T(8,128)} %get-tuple-element.5) | data formatting | bytes 262144

commit v4 on v3

--- a/solution.py
+++ b/solution.py
@@ -165,16 +165,16 @@
 
     def loop_q(body):
         def step(i, c):
-            body(reach - i)
-            body(reach + i)
+            body(i - 1)
+            body(near - i)
             return c
         lax.fori_loop(1, reach + 1, step, 0)
 
     def fetch_start(e, vb):
         ghost_ref[e, reach] = vb
-        for i in range(1, reach + 1):
-            ghost_copy(e, reach - i).start()
-            ghost_copy(e, reach + i).start()
+        for i in range(reach):
+            ghost_copy(e, i).start()
+            ghost_copy(e, near - 1 - i).start()
 
     def transposed(e):
         def one(t):
@@ -209,7 +209,7 @@
         acc = one(reach, tuple(jnp.zeros((rhs, atoms), F32) for _ in range(blocks)))
 
         def step(i, acc):
-            for t in (reach - i, reach + i):
+            for t in (i - 1, near - i):
                 ghost_copy(e, t).wait_recv()
                 acc = one(t, acc)
             return acc

time: 114 us -> 112 us (0.982)
    pallas_call x1, Pallas kernels: 108 us -> 107 us  [local(): pl.pallas_call(functools.partial(kernel, rows_n, near, half), out_shape=(...]
where the time goes in v4:
time: 112 us
  Pallas kernels  107 us (96%)
  local copies, waits for them, and re-layouts  4.41 us (4%)
    pallas_call x1, Pallas kernels, local(): pl.pallas_call(functools.partial(kernel, rows_n, near, half), out_shape=(...  107 us
    unnamed x3, local copies, waits for them, and re-layouts  4.41 us

profile of v4, /device:TPU:0, one launch (start us, length us, event | category | flops | bytes accessed | tf_op | source)
XLA Modules:
  0.0 112.0 jit_solution(9288963559463633679)
XLA Ops:
  0.6 1.3 %copy.12 = s32[1,1,7,8]{3,2,1,0:T(8,128)} copy(s32[1,1,7,8]{3,1,2,0:T(1,128)} %param.15) | data formatting | bytes 448
  1.9 106.9 %shard_map.95 = (f32[8,32,128]{2,1,0:T(8,128)}, f32[8,32,128]{2,1,0:T(8,128)}) custom-call(s32[8,7]{1,0:T(8,128)} %slot_ref.1, s32[7,8]{1,0:T(8,128)} %bitcast.7, f32[8,32,128]{2,1,0:T(8,128)} %pot_hbm.1, f32[8,32,128]{2,1,0:T(8,128)} %guess_hbm.1, bf16[8,128,128]{2,1,0:T(8,128)(2,1)} %ediag_hbm.1, bf16[56,128,128]{2,1,0:T(8,128)(2,1)} %bitcast.5, ...), custom_call_target="tpu_custom_call" | custom-call | tf_op jit(solution)/shard_map/pallas_call | solution.py:367
  108.9 1.6 %copy.15 = f32[8,32,128]{2,1,0:T(8,128)} copy(f32[8,32,128]{2,1,0:T(8,128)} %get-tuple-element.4) | data formatting | bytes 262144
  110.4 1.6 %copy.16 = f32[8,32,128]{2,1,0:T(8,128)} copy(f32[8,32,128]{2,1,0:T(8,128)} %get-tuple-element.5) | data formatting | bytes 262144
